TPU v7x, 128 devices: a whole 4x4x4 slice. The times are simulated.
128 devices in a mesh: dp: 8 (over x, y_hi), seq: 16 (over z, y_lo, core).
Axes of the slice: x: 4, y: 4 (y_hi: 2, y_lo: 2; y = y_hi * 2 + y_lo), z: 4, core: 2. Of those that a mesh axis runs over, the one named last changes fastest.
Arguments:
- tokens: bfloat16 [8, 16, 384, 3072], P('dp', 'seq'), may hold values from -45 to 45
- spatial_query: bfloat16 [8, 16, 384, 1536], P('dp', 'seq'), may hold values from -100 to 100
- spatial_key: bfloat16 [8, 16, 384, 1536], P('dp', 'seq'), may hold values from -6 to 6
- spatial_value: bfloat16 [8, 16, 384, 1536], P('dp', 'seq'), may hold values from -6 to 6
- out_weight: bfloat16 [1536, 3072], P('dp', 'seq'), may hold values from -0.15625 to 0.15625
- qkv_weight: bfloat16 [3072, 4608], P('dp', 'seq'), may hold values from -0.09021098 to 0.09021098
- modulation: float32 [8, 3, 3072], P('dp'), may hold values from -4 to 4
- query_gain: float32 [128], replicated, may hold values from 0.5 to 6
- key_gain: float32 [128], replicated, may hold values from 0.5 to 6
Outputs:
- temporal_out: bfloat16 [8, 16, 384, 1536], P('dp', None, 'seq')
All inputs are finite; a program needn't handle non-finite values.
Results may differ from a plain program's by a relative error of at most 0.025.
Values may be sent and summed in bfloat16 or wider, within the bound.
A program may use at most 128 MiB of HBM per device.

v0:
```python
import jax
import jax.numpy as jnp
from jax import lax
from jax.sharding import PartitionSpec as P


def spatial_frame(query, key, value, heads, head_dim):
    rows = query.shape[0]
    q = query.reshape(rows, heads, head_dim)
    k = key.reshape(rows, heads, head_dim)
    v = value.reshape(rows, heads, head_dim)
    scores = jnp.einsum("ihd,jhd->hij", q, k, preferred_element_type=jnp.float32) / jnp.sqrt(
        jnp.float32(head_dim)
    )
    probs = jax.nn.softmax(scores, axis=-1).astype(jnp.bfloat16)
    attn = jnp.einsum("hij,jhd->ihd", probs, v, preferred_element_type=jnp.float32)
    return attn.astype(jnp.bfloat16).reshape(rows, heads * head_dim)


def head_norm(values, gain):
    wide = values.astype(jnp.float32)
    scale = lax.rsqrt(jnp.mean(wide * wide, axis=-1, keepdims=True) + 1e-06)
    return (wide * scale * gain).astype(jnp.bfloat16)


def temporal(qkv, query_gain, key_gain, head_dim):
    query = head_norm(qkv[:, :, 0], query_gain)
    key = head_norm(qkv[:, :, 1], key_gain)
    value = qkv[:, :, 2]
    scores = jnp.einsum(
        "fphd,gphd->phfg", query, key, preferred_element_type=jnp.float32
    ) / jnp.sqrt(jnp.float32(head_dim))
    probs = jax.nn.softmax(scores, axis=-1).astype(jnp.bfloat16)
    return jnp.einsum("phfg,gphd->fphd", probs, value, preferred_element_type=jnp.float32).astype(
        jnp.bfloat16
    )


def local(
    tokens,
    spatial_query,
    spatial_key,
    spatial_value,
    out_weight,
    qkv_weight,
    modulation,
    query_gain,
    key_gain,
):
    seq_len = tokens.shape[2]
    width = tokens.shape[3]
    head_dim = query_gain.shape[0]
    heads = spatial_query.shape[3] // head_dim
    out_first = lax.all_gather(out_weight, "dp", axis=0, tiled=True)
    spatial = spatial_frame(
        spatial_query[0, 0], spatial_key[0, 0], spatial_value[0, 0], heads, head_dim
    )
    proj = jnp.dot(
        spatial,
        lax.all_gather(out_first, "seq", axis=1, tiled=True),
        preferred_element_type=jnp.float32,
    )
    gate = modulation[0, 0]
    shift = modulation[0, 1]
    scale = modulation[0, 2]
    mixed = (tokens[0, 0].astype(jnp.float32) + gate * proj).astype(jnp.bfloat16)
    wide = mixed.astype(jnp.float32)
    mean = jnp.mean(wide, axis=-1, keepdims=True)
    var = jnp.mean((wide - mean) ** 2, axis=-1, keepdims=True)
    normed = ((wide - mean) * lax.rsqrt(var + 1e-06) * (1.0 + scale) + shift).astype(jnp.bfloat16)
    moved = lax.all_to_all(
        normed.reshape(1, 1, seq_len, width), "seq", split_axis=2, concat_axis=1, tiled=True
    )
    frames = moved.shape[1]
    places = moved.shape[2]
    flat = moved.reshape(frames * places, width)
    qkv_first = lax.all_gather(qkv_weight, "dp", axis=0, tiled=True)
    qkv = jnp.dot(
        flat,
        lax.all_gather(qkv_first, "seq", axis=1, tiled=True),
        preferred_element_type=jnp.float32,
    )
    qkv = qkv.astype(jnp.bfloat16).reshape(frames, places, 3, heads, head_dim)
    result = temporal(qkv, query_gain, key_gain, head_dim)
    return result.reshape(1, frames, places, heads * head_dim)


def solution(mesh):
    placed = (
        P("dp", "seq", None, None),
        P("dp", "seq", None, None),
        P("dp", "seq", None, None),
        P("dp", "seq", None, None),
        P("dp", "seq"),
        P("dp", "seq"),
        P("dp", None, None),
        P(),
        P(),
    )
    return jax.shard_map(
        local, mesh=mesh, in_specs=placed, out_specs=P("dp", None, "seq", None), check_vma=False
    )
```

profile of v0, /device:TPU:1, one launch (start us, length us, event | category | flops | bytes accessed | tf_op | source)
XLA Modules:
  0.0 347.6 jit_solution(1371734036276898651)
XLA Ops:
  6.5 0.0 all-gather.6.cloned.1.call-start
  6.5 0.7 all-gather.6.cloned.1.call-update
  7.3 0.0 copy-start.1
  7.3 0.0 all-gather.4.cloned.1.call-start
  7.3 32.4 %all_gather.12 = bf16[1536,192]{1,0:T(8,128)(2,1)S(1)} all-gather(bf16[192,192]{1,0:T(8,128)(2,1)} %param.13), channel_id=1, replica_groups=mesh['dp'=8,'seq'=16] {'dp'}, dimensions={0}, use_global_device_ids=true | all-gather | bytes 663552 | tf_op jit(solution)/shard_map/all_gather | solution.py:54
  39.7 1.1 copy.61
  40.8 0.0 copy-start.2
  40.8 0.0 all-gather.4.cloned.1.call-update
  40.9 0.0 all-gather.8.cloned.1.call-start
  40.9 25.9 %all-gather.6.cloned.1.call-done = bf16[3072,288]{0,1:T(8,128)(2,1)} async-done(((bf16[384,288]{0,1:T(8,128)(2,1)}), bf16[3072,288]{0,1:T(8,128)(2,1)}) %all-gather.6.cloned.1.call-update) | async-done | bytes 1769488 | tf_op jit(solution)/shard_map/all_gather | solution.py:77
  66.8 0.0 all-gather.8.cloned.1.call-update
  66.8 0.0 copy-done.1
  66.8 1.4 copy.55
  68.3 0.0 copy-done.2
  68.3 0.0 copy-start.3
  68.3 1.4 copy.56
  69.7 0.0 copy-done.3
  69.7 0.0 copy-start.4
  69.7 0.7 copy.59
  70.4 0.5 copy-done.4
  70.9 0.0 copy-start.5
  70.9 6.4 %fusion.37 = (f32[12,384]{1,0:T(8,128)S(1)}, f32[12,384,384]{1,2,0:T(8,128)}) fusion(bf16[384,12,128]{0,2,1:T(8,128)(2,1)S(1)} %bitcast.51, bf16[384,12,128]{0,2,1:T(8,128)(2,1)} %bitcast.52), kind=kOutput, calls=%fused_computation.55 | convolution fusion | flops 458293632 | bytes 9455616 | tf_op jit(solution)/shard_map/sub | solution.py:15
  77.3 0.0 copy-done.5
  77.4 4.1 %fusion.26 = bf16[12,384,128]{1,2,0:T(8,128)(2,1)S(1)} fusion(bf16[384,12,128]{0,2,1:T(8,128)(2,1)S(1)} %bitcast.50, f32[12,384,384]{1,2,0:T(8,128)} %get-tuple-element.13, f32[12,384]{1,0:T(8,128)S(1)} %get-tuple-element.12), kind=kOutput, calls=%fused_computation.38 | convolution fusion | flops 457113600 | bytes 9455616 | tf_op jit(solution)/shard_map/hij,jhd->ihd/dot_general | solution.py:16
  81.4 44.4 %all-gather.4.cloned.1.call-done = bf16[1536,3072]{0,1:T(8,128)(2,1)} async-done(((bf16[1536,192]{0,1:T(8,128)(2,1)}), bf16[1536,3072]{0,1:T(8,128)(2,1)}) %all-gather.4.cloned.1.call-update) | async-done | bytes 9437200 | tf_op jit(solution)/shard_map/all_gather | solution.py:60
  125.8 14.0 %convert_reduce_fusion = (f32[384]{0:T(512)S(1)}, bf16[384,3072]{1,0:T(8,128)(2,1)S(1)}) fusion(bf16[384,1536]{0,1:T(8,128)(2,1)S(1)} %bitcast.56, bf16[1536,3072]{0,1:T(8,128)(2,1)} %all-gather.4.cloned.1.call-done, f32[3072]{0:T(1024)S(1)} %bitcast.55, bf16[1,1,384,3072]{3,2,1,0:T(8,128)(2,1)} %param.9), kind=kOutput, calls=%fused_computation.8 | convolution fusion | flops 3630956032 | bytes 15349248 | tf_op jit(solution)/shard_map/dot_general | solution.py:58
  139.8 0.8 fusion.5
  140.6 1.2 fusion.20
  141.9 5.8 %copy.85 = bf16[1,1,384,3072]{3,1,0,2:T(2,128)(2,1)} copy(bf16[1,1,384,3072]{3,2,1,0:T(8,128)(2,1)S(1)} %fusion.20) | data formatting | bytes 4718592 | tf_op jit(solution)/shard_map/reshape | solution.py:72
  147.6 0.5 broadcast.71
  148.2 14.3 %reduce = bf16[384,3072]{1,0:T(8,128)(2,1)S(1)} reduce(bf16[384,1,1,3072]{3,2,1,0:T(2,128)(2,1)} %bitcast.48, bf16[]{:T(256)} %broadcast.71), dimensions={1,2}, to_apply=%bitcast.47.reduce_sub_computation | reduce | bytes 4718594
  162.4 2.8 reshape.76
  165.2 60.2 %all_to_all.4 = bf16[16,2,36864]{2,1,0:T(2,128)(2,1)S(1)} all-to-all(bf16[16,2,36864]{2,1,0:T(2,128)(2,1)} %reshape.76), channel_id=1, replica_groups=mesh['dp'=8,'seq'=16] {'seq'}, dimensions={0} | all-to-all | bytes 4718592 | tf_op jit(solution)/shard_map/all_to_all | solution.py:71
  225.4 7.0 %reshape.77 = bf16[384,1,1,3072]{3,2,1,0:T(2,128)(2,1)} reshape(bf16[16,2,36864]{2,1,0:T(2,128)(2,1)S(1)} %all_to_all.4) | data formatting | bytes 4718592
  232.4 67.4 %all-gather.8.cloned.1.call-done = bf16[3072,4608]{0,1:T(8,128)(2,1)} async-done(((bf16[3072,288]{0,1:T(8,128)(2,1)}), bf16[3072,4608]{0,1:T(8,128)(2,1)}) %all-gather.8.cloned.1.call-update) | async-done | bytes 28311568 | tf_op jit(solution)/shard_map/all_gather | solution.py:80
  299.8 16.7 %convolution_convert_fusion = bf16[384,4608]{1,0:T(8,128)(2,1)S(1)} fusion(bf16[3072,4608]{0,1:T(8,128)(2,1)} %all-gather.8.cloned.1.call-done, bf16[1,1,384,3072]{3,1,0,2:T(2,128)(2,1)} %bitcast.49), kind=kOutput, calls=%fused_computation.4 | convolution fusion | flops 10873405440 | bytes 34209792 | tf_op jit(solution)/shard_map/dot_general | solution.py:78
  316.5 4.4 %reshape.71 = bf16[16,24,3,12,128]{4,3,2,1,0:T(8,128)(2,1)} reshape(bf16[384,4608]{1,0:T(8,128)(2,1)S(1)} %convolution_convert_fusion) | data formatting | bytes 7077888 | tf_op jit(solution)/shard_map/reshape | solution.py:83
  320.8 0.0 copy-start
  320.8 3.8 %fusion.14 = (f32[16,24,12]{2,1,0:T(8,128)S(1)}, f32[16,24,12]{2,1,0:T(8,128)S(1)}) fusion(bf16[16,24,3,12,128]{4,3,2,1,0:T(8,128)(2,1)} %reshape.71), kind=kLoop, calls=%fused_computation.23 | loop fusion | flops 3529728 | bytes 2396160 | tf_op jit(solution)/shard_map/reduce_sum | solution.py:22
  324.6 0.0 copy-start.6
  324.7 0.0 copy-start.7
  324.7 0.1 add_rsqrt_fusion
  324.7 0.0 copy-done
  324.7 0.6 copy-done.6
  325.3 0.0 copy-done.7
  325.3 1.9 fusion.16
  327.3 1.5 fusion.28
  328.7 0.0 slice-start
  328.7 9.3 %fusion.38 = (f32[24,12,16]{2,1,0:T(8,128)S(1)}, f32[24,12,16,16]{2,3,1,0:T(8,128)S(1)}) fusion(f32[24,12,16,16]{2,3,1,0:T(8,128)S(1)} %fusion.28), kind=kOutput, calls=%fused_computation.56 | output fusion | flops 294927 | bytes 608256 | tf_op jit(solution)/shard_map/sub | solution.py:33
  338.0 0.0 slice-done
  338.0 1.0 fusion.27
  339.0 0.4 copy.67
  339.4 1.6 reshape.72
  (3 shorter events, 0.0 us)
Async XLA Ops:
  6.5 60.3 %all-gather.6.cloned.1.call-start = ((), (), s32[]{:S(2)}) async-start(), calls=%async_computation.2 | async-start | bytes 1990656 | tf_op jit(solution)/shard_map/all_gather | solution.py:77
  7.3 59.6 %copy-start.1 = (bf16[1,1,384,1536]{3,2,1,0:T(8,128)(2,1)S(1)}, bf16[1,1,384,1536]{3,2,1,0:T(8,128)(2,1)}, u32[]{:S(2)}) copy-start(bf16[1,1,384,1536]{3,2,1,0:T(8,128)(2,1)} %param.10) | copy-start | bytes 3538948
  7.3 118.5 %all-gather.4.cloned.1.call-start = ((), (), s32[]{:S(2)}) async-start(), calls=%async_computation.1 | async-start | bytes 10027008 | tf_op jit(solution)/shard_map/all_gather | solution.py:60
  40.8 27.4 %copy-start.2 = (bf16[1,1,384,1536]{3,2,1,0:T(8,128)(2,1)S(1)}, bf16[1,1,384,1536]{3,2,1,0:T(8,128)(2,1)}, u32[]{:S(2)}) copy-start(bf16[1,1,384,1536]{3,2,1,0:T(8,128)(2,1)} %param.11) | copy-start | bytes 3538948
  40.9 259.0 %all-gather.8.cloned.1.call-start = ((), (), s32[]{:S(2)}) async-start(), calls=%async_computation.3 | async-start | bytes 30081024 | tf_op jit(solution)/shard_map/all_gather | solution.py:80
  68.3 1.4 copy-start.3
  69.7 1.3 copy-start.4
  70.9 6.4 %copy-start.5 = (f32[1,3,3072]{2,0,1:T(1,128)S(1)}, f32[1,3,3072]{2,0,1:T(1,128)}, u32[]{:S(2)}) copy-start(f32[1,3,3072]{2,0,1:T(1,128)} %param.15) | copy-start | bytes 110596
  320.8 3.9 %copy-start = (bf16[16,24,3,12,128]{4,3,2,1,0:T(8,128)(2,1)S(1)}, bf16[16,24,3,12,128]{4,3,2,1,0:T(8,128)(2,1)}, u32[]{:S(2)}) copy-start(bf16[16,24,3,12,128]{4,3,2,1,0:T(8,128)(2,1)} %reshape.71) | copy-start | bytes 10616836
  324.6 0.7 copy-start.6
  324.7 0.7 copy-start.7
  328.7 9.3 %slice-start = ((bf16[16,24,3,12,128]{4,3,2,1,0:T(8,128)(2,1)}), bf16[16,24,1,12,128]{4,3,2,1,0:T(8,128)(2,1)S(1)}, s32[]{:S(2)}) async-start(bf16[16,24,3,12,128]{4,3,2,1,0:T(8,128)(2,1)} %reshape.71), calls=%async_computation.4 | async-start | bytes 3145728 | tf_op jit(solution)/shard_map/slice | solution.py:29
Sparse Core Ops, SparseCore 0:
  9.5 57.2 all-gather.5
  68.5 57.2 all-gather.3
  127.5 172.2 all-gather.7
where the time goes:
time: 348 us
  waiting for transfers between devices  138 us (40%)
  blocking collectives  92.6 us (27%)
  matrix products  43.6 us (13%)
  other arithmetic  31.4 us (9%)
  local copies, waits for them, and re-layouts  28.3 us (8%)
  between operations  13.3 us (4%)
    all_gather x1, waiting for transfers between devices, local(): lax.all_gather(qkv_first, 'seq', axis=1, tiled=True)  67.4 us
    all_to_all x1, blocking collectives, local(): lax.all_to_all(normed.reshape(1, 1, seq_len, width), 'seq', split_axis=2,...  60.2 us
    all_gather x1, waiting for transfers between devices, local(): lax.all_gather(out_first, 'seq', axis=1, tiled=True)  44.4 us
    all_gather x1, blocking collectives, local(): out_first = lax.all_gather(out_weight, 'dp', axis=0, tiled=True)  32.4 us
    all_gather x1, waiting for transfers between devices, local(): qkv_first = lax.all_gather(qkv_weight, 'dp', axis=0, tiled=True)  25.9 us
    dot_general x1, matrix products, local(): jnp.dot(flat, lax.all_gather(qkv_first, 'seq', axis=1, tiled=True), prefe...  16.7 us
    unnamed x22, local copies, waits for them, and re-layouts  15 us
    unnamed x1, other arithmetic  14.3 us
  transfers between devices with their start and end apart: 3, of which 3 were waited for; matrix products, arithmetic and copies ran while one was open for 18% of the time, Pallas kernels for 0%

commit v1 on v0

v1 whole, which is shorter than its diff:
```python
import functools

import jax
import jax.numpy as jnp
from jax import lax
from jax.experimental import pallas as pl
from jax.experimental.pallas import tpu as pltpu
from jax.sharding import PartitionSpec as P

MESH = pl.DeviceIdType.MESH
BF = jnp.bfloat16
F32 = jnp.float32

W_PIECES = (("yzx", 0, 112, 64), ("zxy", 112, 96, 48), ("xyz", 208, 80, 48))
O_PIECES = (("yzx", 0, 32, 16), ("zxy", 32, 32, 16), ("xyz", 64, 32, 16))


def dot(a, b):
    return jnp.dot(a, b, preferred_element_type=F32)


def kernel(
    q_hbm, k_hbm, v_hbm, tok_hbm, ow, wt, mod, qg, kg, out_hbm,
    wbuf, obuf, acc, tok, qs, ks, vs, mix, moved, xt, ot, oin,
    load_sem, out_sem, ring_s, ring_r, near_s, near_r, oin_s, oin_r, a2a_s, a2a_r, fwd_s, fwd_r,
):
    dp = lax.axis_index("dp")
    seq = lax.axis_index("seq")
    x, z, c = dp // 2, seq // 4, seq % 2
    yl = (seq // 2) % 2
    y = (dp % 2) * 2 + yl
    me = {"x": x, "y": y, "z": z}
    chip = z * 2 + yl

    def device(at, core):
        return (at["x"] * 2 + at["y"] // 2, at["z"] * 4 + (at["y"] % 2) * 2 + core)

    def step(axis, by):
        return {**me, axis: lax.rem(me[axis] + by, 4)}

    def other_chip(t):
        return (dp, t * 2 + c)

    near = device(me, 1 - c)

    loads = [
        pltpu.make_async_copy(src, dst, load_sem.at[i])
        for i, (src, dst) in enumerate(((q_hbm, qs), (k_hbm, ks), (v_hbm, vs), (tok_hbm, tok)))
    ]
    for copy in loads:
        copy.start()

    wbuf[x, z, y, c] = wt[...]

    barrier = pltpu.get_barrier_semaphore()
    partners = [device(step(a, by), c) for a in "xyz" for by in (1, 3)] + [near]
    partners += [other_chip(lax.rem(chip + 2 * k, 8)) for k in (2,)]
    flip = z * 2 + (1 - yl)
    partners += [other_chip(lax.rem(flip + 2 * k, 8)) for k in (1, 2, 3)]
    for partner in partners:
        pl.semaphore_signal(barrier, inc=1, device_id=partner, device_id_type=MESH)
    pl.semaphore_wait(barrier, len(partners))

    pending = []

    def remote(src, dst, send, recv, to):
        return pltpu.make_async_remote_copy(
            src_ref=src, dst_ref=dst, send_sem=send, recv_sem=recv, device_id=to, device_id_type=MESH
        )

    def start(src, dst, send, recv, to):
        copy = remote(src, dst, send, recv, to)
        copy.start()
        pending.append(copy)

    def slot(buf, order, phase, shift, core, r0, n):
        index = {}
        for i, axis in enumerate(order):
            if i < phase:
                index[axis] = slice(None)
            elif i == phase:
                index[axis] = lax.rem(me[axis] + shift, 4)
            else:
                index[axis] = me[axis]
        return buf.at[index["x"], index["z"], index["y"], core, pl.ds(r0, n), :]

    class Piece:
        def __init__(self, buf, spec, base):
            self.buf = buf
            self.order, self.r0, self.n, self.half = spec
            self.base = base

        def part(self, phase, shift, which):
            r0, n = {
                "A": (self.r0, self.half),
                "B": (self.r0 + self.half, self.n - self.half),
                "W": (self.r0, self.n),
            }[which]
            return slot(self.buf, self.order, phase, shift, c, r0, n)

        def send(self, phase, way, k, shift, which):
            ref = self.part(phase, shift, which)
            i = self.base * 3 + phase
            to = device(step(self.order[phase], (1, 3)[way]), c)
            start(ref, ref, ring_s.at[i, way, k], ring_r.at[i, way, k], to)

        def wait(self, phase, way, k, shift, which):
            ref = self.part(phase, shift, which)
            i = self.base * 3 + phase
            remote(ref, ref, ring_s.at[i, way, k], ring_r.at[i, way, k], near).wait_recv()

        def own(self, phase):
            for way, names in ((0, "AB"), (1, "BA")):
                for k, which in enumerate(names):
                    self.send(phase, way, k, 0, which)

        def forward(self, phase):
            self.wait(phase, 0, 0, 3, "A")
            self.send(phase, 0, 2, 3, "A")
            self.wait(phase, 1, 0, 1, "B")
            self.send(phase, 1, 2, 1, "B")

        def rest(self, phase, sides=True, far=True):
            if sides:
                self.wait(phase, 0, 1, 3, "B")
                self.wait(phase, 1, 1, 1, "A")
            if far:
                self.wait(phase, 0, 2, 2, "A")
                self.wait(phase, 1, 2, 2, "B")

        def to_near(self, shift):
            ref = self.part(2, shift, "W")
            start(ref, ref, near_s.at[self.base, shift], near_r.at[self.base, shift], near)

        def from_near(self, shift):
            ref = slot(self.buf, self.order, 2, shift, 1 - c, self.r0, self.n)
            remote(ref, ref, near_s.at[self.base, shift], near_r.at[self.base, shift], near).wait_recv()

    ws = [Piece(wbuf, spec, i) for i, spec in enumerate(W_PIECES)]
    os = [Piece(obuf, spec, 3 + i) for i, spec in enumerate(O_PIECES)]

    half = ow.at[pl.ds(pl.multiple_of(96 * (1 - c), 16), 96), :]
    start(half, oin, oin_s, oin_r, near)
    for piece in ws:
        piece.own(0)
    row = lax.broadcasted_iota(jnp.int32, (192, 384), 0)
    col = lax.broadcasted_iota(jnp.int32, (192, 384), 1)
    mine = ow[pl.ds(pl.multiple_of(96 * c, 16), 96), :]
    block = dot(mine, (col - row == 192 * c).astype(F32).astype(BF))
    remote(oin, oin, oin_s, oin_r, near).wait_recv()
    block += dot(oin[...], (col - row == 192 * (1 - c)).astype(F32).astype(BF))
    obuf[x, z, y, c] = block.astype(BF)
    for piece in os:
        piece.own(0)

    for copy in loads[:3]:
        copy.wait()

    def heads(first, count):
        def body(h, _):
            cols = pl.ds(pl.multiple_of(h * 128, 128), 128)
            s = lax.dot_general(
                qs[:, cols], ks[:, cols], (((1,), (1,)), ((), ())), preferred_element_type=F32
            )
            s = s * (128**-0.5)
            e = jnp.exp(s - jnp.max(s, axis=1, keepdims=True))
            total = jnp.sum(e, axis=1, keepdims=True)
            o = dot(e.astype(BF), vs[:, cols])
            qs[:, cols] = (o / total).astype(BF)
            return 0

        lax.fori_loop(first, first + count, body, 0)

    heads(0, 2)
    for piece in os:
        piece.forward(0)
    heads(2, 1)
    for piece in os:
        piece.rest(0)
        piece.own(1)
    for piece in ws:
        piece.forward(0)
    heads(3, 2)
    for piece in os:
        piece.forward(1)
    for piece in ws:
        piece.rest(0)
        piece.own(1)
    heads(5, 2)
    for piece in os:
        piece.rest(1)
        piece.own(2)
        piece.to_near(0)
    heads(7, 3)
    for piece in ws:
        piece.forward(1)
    heads(10, 2)
    for piece in os:
        piece.forward(2)
    for piece in ws:
        piece.rest(1)
        piece.own(2)
        piece.to_near(0)
    for piece in os:
        piece.rest(2, far=False)
        piece.to_near(1)
        piece.to_near(3)
    for piece in os:
        piece.rest(2, sides=False)
        piece.to_near(2)
    for piece in os:
        for shift in range(4):
            piece.from_near(shift)
    loads[3].wait()

    def project(zz, _):
        rhs = jnp.concatenate(
            [
                jnp.concatenate(
                    [obuf[xx, zz, yh * 2 + l, cc] for xx in range(4) for yh in range(2) for cc in range(2)],
                    axis=0,
                )
                for l in range(2)
            ],
            axis=1,
        )
        cols = pl.ds(pl.multiple_of(zz * 768, 768), 768)
        proj = dot(qs[...], rhs)
        mix[:, cols] = (tok[:, cols].astype(F32) + mod[0, 0:1, cols] * proj).astype(BF)
        return 0

    lax.fori_loop(0, 4, project, 0)
    for piece in ws:
        piece.forward(2)

    def normed(t):
        rows = pl.ds(pl.multiple_of(t * 48, 16), 48)
        wide = mix[rows, :].astype(F32)
        mean = jnp.mean(wide, axis=1, keepdims=True)
        dev = wide - mean
        var = jnp.mean(dev * dev, axis=1, keepdims=True)
        return rows, (dev * lax.rsqrt(var + 1e-06) * (1.0 + mod[0, 2:3, :]) + mod[0, 1:2, :]).astype(BF)

    def norm_and_send(i, _):
        t = lax.rem(chip + 1 + i, 8)
        rows, value = normed(t)
        mix[rows, :] = value
        remote(mix.at[rows, :], moved.at[seq], a2a_s.at[i], a2a_r.at[i], other_chip(t)).start()
        return 0

    lax.fori_loop(0, 7, norm_and_send, 0)
    moved[seq] = normed(chip)[1]

    def to_near_rows(i):
        t = lax.rem(chip + 7 - i, 8)
        ref = moved.at[t * 2 + c, pl.ds(pl.multiple_of(16 * (1 - c), 16), 32), :]
        return remote(ref, ref, fwd_s.at[i], fwd_r.at[i], near)

    to_near_rows(7).start()

    def pass_on(i, _):
        t = lax.rem(chip + 7 - i, 8)
        ref = moved.at[t * 2 + c]
        remote(ref, ref, a2a_s.at[i], a2a_r.at[i], near).wait_recv()
        to_near_rows(i).start()
        return 0

    lax.fori_loop(0, 7, pass_on, 0)

    def arrive(i, _):
        t = lax.rem(chip + 7 - i, 8)
        ref = moved.at[t * 2 + 1 - c, pl.ds(pl.multiple_of(16 * c, 16), 32), :]
        remote(ref, ref, fwd_s.at[i], fwd_r.at[i], near).wait_recv()
        return 0

    lax.fori_loop(0, 8, arrive, 0)

    m = lax.broadcasted_iota(jnp.int32, (384, 512), 0)
    r = lax.broadcasted_iota(jnp.int32, (384, 512), 1)
    pick = (r == (m & 15) * 32 + (m >> 4) + 8 * c).astype(F32).astype(BF)

    def turn(i, _):
        cols = pl.ds(pl.multiple_of(i * 384, 384), 384)
        rows = moved[:, pl.ds(pl.multiple_of(16 * c, 16), 32), cols].reshape(512, 384)
        xt[cols, :] = dot(pick, rows).astype(BF).T
        return 0

    lax.fori_loop(0, 8, turn, 0)

    def put(rows, value, first):
        if first:
            acc[rows, :] = value
        else:
            acc[rows, :] += value

    def start_row(zz, l, cc, r0):
        return pl.multiple_of(zz * 1152 + l * 576 + cc * 288 + r0, 16)

    def chunk_x(shift):
        _, r0, n, _ = W_PIECES[0]
        xx = lax.rem(x + shift, 4)
        rhs_rows = pl.ds(pl.multiple_of(xx * 768, 768), 768)

        def body(zz, _):
            lhs = jnp.concatenate(
                [
                    jnp.concatenate([wbuf[xx, zz, yh * 2 + l, cc, r0 : r0 + n, :] for yh in range(2)], axis=1)
                    for l in range(2)
                    for cc in range(2)
                ],
                axis=0,
            )
            res = dot(lhs, xt[rhs_rows, :])
            for i in range(4):
                put(pl.ds(start_row(zz, i // 2, i % 2, r0), n), res[i * n : (i + 1) * n], shift == 0)
            return 0

        lax.fori_loop(0, 4, body, 0)

    def chunk_y(shift, first):
        _, r0, n, _ = W_PIECES[1]
        yy = lax.rem(y + shift, 4)
        hi, lo = yy // 2, yy % 2
        rhs = jnp.concatenate(
            [xt[pl.ds(pl.multiple_of(xx * 768 + hi * 384, 384), 384), :] for xx in range(4)], axis=0
        )

        def body(zp, _):
            lhs = jnp.concatenate(
                [
                    jnp.concatenate([wbuf[xx, zp * 2 + zz, yy, cc, r0 : r0 + n, :] for xx in range(4)], axis=1)
                    for zz in range(2)
                    for cc in range(2)
                ],
                axis=0,
            )
            res = dot(lhs, rhs)
            for i in range(4):
                put(pl.ds(start_row(zp * 2 + i // 2, lo, i % 2, r0), n), res[i * n : (i + 1) * n], first)
            return 0

        lax.fori_loop(0, 2, body, 0)

    def chunk_z(shift):
        _, r0, n, _ = W_PIECES[2]
        zz = lax.rem(z + shift, 4)
        lhs = jnp.concatenate(
            [
                jnp.concatenate(
                    [wbuf[xx, zz, yh * 2 + l, cc, r0 : r0 + n, :] for xx in range(4) for yh in range(2)], axis=1
                )
                for l in range(2)
                for cc in range(2)
            ],
            axis=0,
        )
        res = dot(lhs, xt[...])
        for i in range(4):
            put(pl.ds(start_row(zz, i // 2, i % 2, r0), n), res[i * n : (i + 1) * n], True)

    def chunk(shift):
        for piece in ws:
            piece.from_near(shift)
        chunk_x(shift)
        chunk_y(shift, shift < 2)
        chunk_z(shift)

    chunk(0)
    for piece in ws:
        piece.rest(2, far=False)
        piece.to_near(1)
        piece.to_near(3)
    chunk(1)
    chunk(3)
    for piece in ws:
        piece.rest(2, sides=False)
        piece.to_near(2)
    chunk(2)

    def unit(rows, gain):
        wide = acc[rows, :].astype(BF).astype(F32)
        scale = lax.rsqrt(jnp.sum(wide * wide, axis=0, keepdims=True) * (1.0 / 128) + 1e-06)
        return (wide * scale * gain).astype(BF)

    ii = lax.broadcasted_iota(jnp.int32, (128, 128), 0)
    jj = lax.broadcasted_iota(jnp.int32, (128, 128), 1)
    same = (ii >> 4) == (jj >> 4)

    def temporal(h, _):
        rows = pl.multiple_of(h * 128, 128)
        q = unit(pl.ds(rows, 128), qg[...])
        k = unit(pl.ds(1536 + rows, 128), kg[...])
        v = acc[pl.ds(3072 + rows, 128), :].astype(BF)
        for g in range(3):
            cols = slice(g * 128, (g + 1) * 128)
            s = dot(k[:, cols].T, q[:, cols]) * (128**-0.5)
            s = jnp.where(same, s, -1e30)
            e = jnp.exp(s - jnp.max(s, axis=0, keepdims=True))
            p = (e / jnp.sum(e, axis=0, keepdims=True)).astype(BF)
            ot[pl.ds(rows, 128), cols] = dot(v[:, cols], p).astype(BF)
        return 0

    lax.fori_loop(0, 12, temporal, 0)

    a = lax.broadcasted_iota(jnp.int32, (384, 384), 0)
    b = lax.broadcasted_iota(jnp.int32, (384, 384), 1)
    back = (a == (b & 15) * 24 + (b >> 4)).astype(F32).astype(BF)

    def untangle(i, _):
        cols = pl.ds(pl.multiple_of(i * 384, 384), 384)
        ks[:, cols] = lax.dot_general(
            back, ot[cols, :], (((1,), (1,)), ((), ())), preferred_element_type=F32
        ).astype(BF)
        return 0

    lax.fori_loop(0, 4, untangle, 0)
    done = pltpu.make_async_copy(ks, out_hbm, out_sem)
    done.start()

    for copy in pending:
        copy.wait_send()

    def sent(i, _):
        t = lax.rem(chip + 1 + i, 8)
        rows = pl.ds(pl.multiple_of(t * 48, 16), 48)
        remote(mix.at[rows, :], moved.at[seq], a2a_s.at[i], a2a_r.at[i], other_chip(t)).wait_send()
        return 0

    lax.fori_loop(0, 7, sent, 0)

    def sent_near(i, _):
        to_near_rows(i).wait_send()
        return 0

    lax.fori_loop(0, 8, sent_near, 0)
    done.wait()


def local(
    tokens, spatial_query, spatial_key, spatial_value, out_weight, qkv_weight, modulation, query_gain, key_gain
):
    hbm = pl.BlockSpec(memory_space=pl.ANY)
    vmem = pl.BlockSpec(memory_space=pltpu.VMEM)
    dma = pltpu.SemaphoreType.DMA
    out = pl.pallas_call(
        kernel,
        out_shape=jax.ShapeDtypeStruct((384, 1536), BF),
        in_specs=[hbm] * 4 + [vmem] * 5,
        out_specs=hbm,
        scratch_shapes=[
            pltpu.VMEM((4, 4, 4, 2, 288, 384), BF),
            pltpu.VMEM((4, 4, 4, 2, 96, 384), BF),
            pltpu.VMEM((4608, 384), F32),
            pltpu.VMEM((384, 3072), BF),
            pltpu.VMEM((384, 1536), BF),
            pltpu.VMEM((384, 1536), BF),
            pltpu.VMEM((384, 1536), BF),
            pltpu.VMEM((384, 3072), BF),
            pltpu.VMEM((16, 48, 3072), BF),
            pltpu.VMEM((3072, 384), BF),
            pltpu.VMEM((1536, 384), BF),
            pltpu.VMEM((96, 192), BF),
            dma((4,)),
            dma,
            dma((18, 2, 3)),
            dma((18, 2, 3)),
            dma((6, 4)),
            dma((6, 4)),
            dma,
            dma,
            dma((7,)),
            dma((7,)),
            dma((8,)),
            dma((8,)),
        ],
        compiler_params=pltpu.CompilerParams(
            collective_id=0, has_side_effects=True, vmem_limit_bytes=64 * 2**20 - 65536 * 4
        ),
        name="video_block",
    )(
        spatial_query.reshape(384, 1536),
        spatial_key.reshape(384, 1536),
        spatial_value.reshape(384, 1536),
        tokens.reshape(384, 3072),
        out_weight,
        qkv_weight.T,
        modulation,
        query_gain.reshape(128, 1),
        key_gain.reshape(128, 1),
    )
    return out.reshape(1, 16, 24, 1536)


def solution(mesh):
    placed = (
        P("dp", "seq", None, None),
        P("dp", "seq", None, None),
        P("dp", "seq", None, None),
        P("dp", "seq", None, None),
        P("dp", "seq"),
        P("dp", "seq"),
        P("dp", None, None),
        P(),
        P(),
    )
    return jax.shard_map(
        local, mesh=mesh, in_specs=placed, out_specs=P("dp", None, "seq", None), check_vma=False
    )
```

time: 348 us -> 164 us (0.47)
  Pallas kernels: 0 us -> 157 us
  waiting for transfers between devices: 138 us -> 0 us
  blocking collectives: 92.6 us -> 0 us
  matrix products: 43.6 us -> 0 us
  other arithmetic: 31.4 us -> 0 us
  local copies, waits for them, and re-layouts: 28.3 us -> 6.52 us
  between operations: 13.3 us -> 0.01 us
    pallas_call x0 -> x1, Pallas kernels: none -> 157 us  [local(): pl.pallas_call(kernel, out_shape=jax.ShapeDtypeStruct((384, 1536), BF), i...]
    all_gather x3 -> x0, waiting for transfers between devices: 138 us -> none  [the longest x1 67.4 us: local(): lax.all_gather(qkv_first, 'seq', axis=1, tiled=True)]
    all_to_all x1 -> x0, blocking collectives: 60.2 us -> none  [local(): lax.all_to_all(normed.reshape(1, 1, seq_len, width), 'seq', split_axis=2,...]
    dot_general x5 -> x0, matrix products: 37.2 us -> none  [the longest x1 16.7 us: local(): jnp.dot(flat, lax.all_gather(qkv_first, 'seq', axis=1, tiled=True), prefe...]
    all_gather x1 -> x0, blocking collectives: 32.4 us -> none  [local(): out_first = lax.all_gather(out_weight, 'dp', axis=0, tiled=True)]
    unnamed x1 -> x0, other arithmetic: 14.3 us -> none
    unnamed x22 -> x2, local copies, waits for them, and re-layouts: 15 us -> 3.76 us
    sub x1 -> x0, other arithmetic: 9.27 us -> none  [temporal(): probs = jax.nn.softmax(scores, axis=-1).astype(jnp.bfloat16)]
  transfers between devices with their start and end apart: 3 -> 0, of which waited for: 3 -> 0; matrix products, arithmetic and copies ran while one was open for 18% -> 0% of each run, Pallas kernels for 0% -> 0%
where the time goes in v1:
time: 164 us
  Pallas kernels  157 us (96%)
  local copies, waits for them, and re-layouts  6.52 us (4%)
    pallas_call x1, Pallas kernels, local(): pl.pallas_call(kernel, out_shape=jax.ShapeDtypeStruct((384, 1536), BF), i...  157 us
    unnamed x2, local copies, waits for them, and re-layouts  3.76 us

profile of v1, /device:TPU:1, one launch (start us, length us, event | category | flops | bytes accessed | tf_op | source)
XLA Modules:
  0.0 164.0 jit_solution(5249726722503074802)
XLA Ops:
  0.0 1.4 copy.10.mod
  1.4 1.4 copy.11.qg
  2.8 1.4 copy.12.kg
  4.2 157.5 %video_block.1 = bf16[384,1536]{1,0:T(8,128)(2,1)} custom-call(bf16[384,1536]{1,0:T(8,128)(2,1)} %bitcast.10, bf16[384,1536]{1,0:T(8,128)(2,1)} %bitcast.11, bf16[384,1536]{1,0:T(8,128)(2,1)} %bitcast.12, bf16[384,3072]{1,0:T(8,128)(2,1)} %bitcast.9, bf16[192,192]{1,0:T(8,128)(2,1)} %ow.1, bf16[288,384]{1,0:T(8,128)(2,1)} %bitcast.13, ...), custom_call_target="tpu_custom_call" | custom-call | tf_op jit(solution)/shard_map/video_block/pallas_call | solution.py:445
  161.7 2.4 %copy.14 = bf16[1,16,24,1536]{3,2,1,0:T(8,128)(2,1)} copy(bf16[1,16,24,1536]{3,2,1,0:T(8,128)(2,1)} %bitcast.8) | data formatting | bytes 2359296

commit v2 on v1

v2 whole, which is shorter than its diff:
```python
import functools

import jax
import jax.numpy as jnp
from jax import lax
from jax.experimental import pallas as pl
from jax.experimental.pallas import tpu as pltpu
from jax.sharding import PartitionSpec as P

MESH = pl.DeviceIdType.MESH
BF = jnp.bfloat16
F32 = jnp.float32

W_PIECES = (("yzx", 0, 128, 64), ("zxy", 128, 96, 48), ("xyz", 224, 64, 32))
O_PIECES = (("yzx", 0, 32, 16), ("zxy", 32, 32, 16), ("xyz", 64, 32, 16))


def dot(a, b):
    return jnp.dot(a, b, preferred_element_type=F32)


def kernel(
    q_hbm, k_hbm, v_hbm, tok_hbm, ow_hbm, wt_hbm, mod_hbm, qg_hbm, kg_hbm, ot,
    ow, mods, mod, qg, kg, wbuf, obuf, acc, tok, qs, ks, vs, mix, moved, xt, oin,
    load_sem, ring_s, ring_r, near_s, near_r, oin_s, oin_r, a2a_s, a2a_r, fwd_s, fwd_r,
):
    dp = lax.axis_index("dp")
    seq = lax.axis_index("seq")
    x, z, c = dp // 2, seq // 4, seq % 2
    yl = (seq // 2) % 2
    y = (dp % 2) * 2 + yl
    me = {"x": x, "y": y, "z": z}
    chip = z * 2 + yl

    def device(at, core):
        return (at["x"] * 2 + at["y"] // 2, at["z"] * 4 + (at["y"] % 2) * 2 + core)

    def step(axis, by):
        return {**me, axis: lax.rem(me[axis] + by, 4)}

    def other_chip(t):
        return (dp, t * 2 + c)

    near = device(me, 1 - c)

    parts = (
        (ow_hbm, ow), (wt_hbm, wbuf.at[x, z, y, c]), (q_hbm, qs), (k_hbm, ks), (v_hbm, vs), (tok_hbm, tok),
        (mod_hbm, mods), (qg_hbm, qg), (kg_hbm, kg),
    )
    loads = [pltpu.make_async_copy(src, dst, load_sem.at[i]) for i, (src, dst) in enumerate(parts)]
    for copy in loads:
        copy.start()

    barrier = pltpu.get_barrier_semaphore()
    partners = [device(step(a, by), c) for a in "xyz" for by in (1, 2, 3)] + [near]
    flip = z * 2 + (1 - yl)
    partners += [other_chip(lax.rem(flip + 2 * k, 8)) for k in (1, 2, 3)]
    for partner in partners:
        pl.semaphore_signal(barrier, inc=1, device_id=partner, device_id_type=MESH)
    pl.semaphore_wait(barrier, len(partners))
    loads[0].wait()
    loads[1].wait()

    pending = []

    def remote(src, dst, send, recv, to):
        return pltpu.make_async_remote_copy(
            src_ref=src, dst_ref=dst, send_sem=send, recv_sem=recv, device_id=to, device_id_type=MESH
        )

    def start(src, dst, send, recv, to):
        copy = remote(src, dst, send, recv, to)
        copy.start()
        pending.append(copy)

    def shift(axis, part):
        if axis == "y":
            return (0, 1 + 2 * yl, 3 - 2 * yl, 2)[part]
        return (0, 3, 1, 2)[part]

    def to(axis, way):
        by = (1 + 2 * yl, 3 - 2 * yl)[way] if axis == "y" else (1, 3)[way]
        return device(step(axis, by), c)

    class Piece:
        def __init__(self, buf, spec, base):
            self.buf = buf
            self.order, self.r0, self.n, self.half = spec
            self.base = base

        def slot(self, phase, part, rows="W", group=None, core=None):
            at = dict(me)
            for axis in self.order[:phase]:
                at[axis] = slice(None)
            axis = self.order[phase]
            at[axis] = lax.rem(me[axis] + shift(axis, part), 4)
            if group is not None:
                second = self.order[1]
                at[second] = lax.rem(me[second] + shift(second, group), 4)
            r0, n = {
                "A": (self.r0, self.half),
                "B": (self.r0 + self.half, self.n - self.half),
                "W": (self.r0, self.n),
            }[rows]
            return self.buf.at[at["x"], at["z"], at["y"], c if core is None else core, pl.ds(r0, n), :]

        def sem(self, i):
            return ring_s.at[self.base, i], ring_r.at[self.base, i]

        def send(self, ref, i, target):
            start(ref, ref, *self.sem(i), target)

        def wait(self, ref, i):
            remote(ref, ref, *self.sem(i), near).wait_recv()

        def first(self):
            axis = self.order[0]
            ref = self.slot(0, 0)
            self.send(ref, 0, to(axis, 0))
            self.send(ref, 1, to(axis, 1))
            self.send(ref, 2, device(step(axis, 2), c))

        def first_done(self):
            for part in (1, 2, 3):
                self.wait(self.slot(0, part), part - 1)

        def second(self):
            axis = self.order[1]
            for k in range(2):
                for way in range(2):
                    self.send(self.slot(1, 0, "AB"[(way + k) % 2]), 3 + way * 3 + k, to(axis, way))

        def second_on(self):
            axis = self.order[1]
            for way in range(2):
                came = 1 - way if axis == "y" else way
                ref = self.slot(1, 1 + came, "AB"[came])
                self.wait(ref, 3 + came * 3)
                self.send(ref, 3 + way * 3 + 2, to(axis, way))

        def second_sides(self):
            for way in range(2):
                self.wait(self.slot(1, 1 + way, "BA"[way]), 3 + way * 3 + 1)

        def second_far(self):
            axis = self.order[1]
            for way in range(2):
                came = 1 - way if axis == "y" else way
                self.wait(self.slot(1, 3, "AB"[came]), 3 + way * 3 + 2)

        def third(self, group):
            axis = self.order[2]
            for way in range(2):
                self.send(self.slot(2, 0, group=group), 9 + way * 4 + group, to(axis, way))

        def relays(self, way):
            if self.order[2] == "y":
                return ((), (0, 1, 2, 3))[way]
            return ((0, 1), (2, 3))[way]

        def third_on(self, group):
            axis = self.order[2]
            for way in range(2):
                came = 1 - way if axis == "y" else way
                ref = self.slot(2, 1 + came, group=group)
                self.wait(ref, 9 + came * 4 + group)
                if group in self.relays(way):
                    self.send(ref, 17 + way * 4 + group, to(axis, way))

        def third_far(self, group):
            way = 0 if group in self.relays(0) else 1
            self.wait(self.slot(2, 3, group=group), 17 + way * 4 + group)

        def across(self, part, group=None):
            i = part if group is None else 3 + group
            ref = self.slot(2, part, group=group)
            start(ref, ref, near_s.at[self.base, i], near_r.at[self.base, i], near)

        def crossed(self, part, group=None):
            i = part if group is None else 3 + group
            ref = self.slot(2, part, group=group, core=1 - c)
            remote(ref, ref, near_s.at[self.base, i], near_r.at[self.base, i], near).wait_recv()

    ws = [Piece(wbuf, spec, i) for i, spec in enumerate(W_PIECES)]
    os = [Piece(obuf, spec, 3 + i) for i, spec in enumerate(O_PIECES)]

    def each(pieces, name, *args):
        for piece in pieces:
            getattr(piece, name)(*args)

    half = ow.at[pl.ds(pl.multiple_of(96 * (1 - c), 16), 96), :]
    start(half, oin, oin_s, oin_r, near)
    each(ws, "first")
    row = lax.broadcasted_iota(jnp.int32, (192, 384), 0)
    col = lax.broadcasted_iota(jnp.int32, (192, 384), 1)
    mine = ow[pl.ds(pl.multiple_of(96 * c, 16), 96), :]
    block = dot(mine, (col - row == 192 * c).astype(F32).astype(BF))
    remote(oin, oin, oin_s, oin_r, near).wait_recv()
    block += dot(oin[...], (col - row == 192 * (1 - c)).astype(F32).astype(BF))
    obuf[x, z, y, c] = block.astype(BF)
    each(os, "first")

    for copy in loads[2:5]:
        copy.wait()

    def heads(first, count):
        def body(h, _):
            cols = pl.ds(pl.multiple_of(h * 128, 128), 128)
            s = lax.dot_general(
                qs[:, cols], ks[:, cols], (((1,), (1,)), ((), ())), preferred_element_type=F32
            )
            s = s * (128**-0.5)
            e = jnp.exp(s - jnp.max(s, axis=1, keepdims=True))
            total = jnp.sum(e, axis=1, keepdims=True)
            o = dot(e.astype(BF), vs[:, cols])
            qs[:, cols] = (o / total).astype(BF)
            return 0

        lax.fori_loop(first, first + count, body, 0)

    heads(0, 2)
    each(os, "first_done")
    each(os, "second")
    each(os, "third", 0)
    each(ws, "first_done")
    each(ws, "second")
    heads(2, 2)
    each(os, "second_on")
    heads(4, 2)
    each(os, "second_sides")
    each(os, "third", 1)
    each(os, "third", 2)
    each(ws, "second_on")
    heads(6, 2)
    each(os, "second_far")
    each(os, "third", 3)
    each(os, "across", 0)
    each(ws, "third", 0)
    heads(8, 2)
    each(os, "third_on", 0)
    heads(10, 2)
    each(os, "third_on", 1)
    each(os, "third_on", 2)
    each(ws, "second_sides")
    each(ws, "second_far")
    each(os, "third_on", 3)
    for group in (1, 2, 3):
        each(ws, "third", group)
    each(os, "across", 1)
    each(os, "across", 2)
    for group in range(4):
        each(os, "third_far", group)
        each(os, "across", 3, group)
    each(ws, "across", 0)
    for part in range(3):
        each(os, "crossed", part)
    for group in range(4):
        each(os, "crossed", 3, group)
    loads[5].wait()
    loads[6].wait()
    for i in range(72):
        mod[i // 24 : i // 24 + 1, i % 24 * 128 : (i % 24 + 1) * 128] = mods[i : i + 1, :]

    def project(zz, _):
        rhs = jnp.concatenate(
            [
                jnp.concatenate(
                    [obuf[xx, zz, yh * 2 + l, cc] for xx in range(4) for yh in range(2) for cc in range(2)],
                    axis=0,
                )
                for l in range(2)
            ],
            axis=1,
        )
        cols = pl.ds(pl.multiple_of(zz * 768, 768), 768)
        proj = dot(qs[...], rhs)
        mix[:, cols] = (tok[:, cols].astype(F32) + mod[0:1, cols] * proj).astype(BF)
        return 0

    lax.fori_loop(0, 4, project, 0)
    each(ws, "third_on", 0)

    def normed(t):
        rows = pl.ds(pl.multiple_of(t * 48, 16), 48)
        wide = mix[rows, :].astype(F32)
        mean = jnp.mean(wide, axis=1, keepdims=True)
        dev = wide - mean
        var = jnp.mean(dev * dev, axis=1, keepdims=True)
        return rows, (dev * lax.rsqrt(var + 1e-06) * (1.0 + mod[2:3, :]) + mod[1:2, :]).astype(BF)

    def norm_and_send(i, _):
        t = lax.rem(chip + 1 + i, 8)
        rows, value = normed(t)
        mix[rows, :] = value
        remote(mix.at[rows, :], moved.at[seq], a2a_s.at[i], a2a_r.at[i], other_chip(t)).start()
        return 0

    lax.fori_loop(0, 7, norm_and_send, 0)
    each(ws, "third_on", 1)
    each(ws, "third_on", 2)
    moved[seq] = normed(chip)[1]

    def to_near_rows(i):
        t = lax.rem(chip + 7 - i, 8)
        ref = moved.at[t * 2 + c, pl.ds(pl.multiple_of(16 * (1 - c), 16), 32), :]
        return remote(ref, ref, fwd_s.at[i], fwd_r.at[i], near)

    to_near_rows(7).start()
    each(ws, "third_on", 3)
    each(ws, "across", 1)
    each(ws, "across", 2)

    def pass_on(i, _):
        t = lax.rem(chip + 7 - i, 8)
        ref = moved.at[t * 2 + c]
        remote(ref, ref, a2a_s.at[i], a2a_r.at[i], near).wait_recv()
        to_near_rows(i).start()
        return 0

    lax.fori_loop(0, 7, pass_on, 0)

    def arrive(i, _):
        t = lax.rem(chip + 7 - i, 8)
        ref = moved.at[t * 2 + 1 - c, pl.ds(pl.multiple_of(16 * c, 16), 32), :]
        remote(ref, ref, fwd_s.at[i], fwd_r.at[i], near).wait_recv()
        return 0

    lax.fori_loop(0, 8, arrive, 0)

    m = lax.broadcasted_iota(jnp.int32, (384, 512), 0)
    r = lax.broadcasted_iota(jnp.int32, (384, 512), 1)
    pick = (r == (m & 15) * 32 + (m >> 4) + 8 * c).astype(F32).astype(BF)

    def turn(i, _):
        cols = pl.ds(pl.multiple_of(i * 384, 384), 384)
        rows = moved[:, pl.ds(pl.multiple_of(16 * c, 16), 32), cols].reshape(512, 384)
        xt[cols, :] = dot(pick, rows).astype(BF).T
        return 0

    lax.fori_loop(0, 8, turn, 0)

    def put(rows, value, first):
        if first:
            acc[rows, :] = value
        else:
            acc[rows, :] += value

    def start_row(zz, l, cc, r0):
        return pl.multiple_of(zz * 1152 + l * 576 + cc * 288 + r0, 16)

    def chunk_x(part):
        _, r0, n, _ = W_PIECES[0]
        xx = lax.rem(x + shift("x", part), 4)
        rhs_rows = pl.ds(pl.multiple_of(xx * 768, 768), 768)

        def body(zz, _):
            lhs = jnp.concatenate(
                [
                    jnp.concatenate([wbuf[xx, zz, yh * 2 + l, cc, r0 : r0 + n, :] for yh in range(2)], axis=1)
                    for l in range(2)
                    for cc in range(2)
                ],
                axis=0,
            )
            res = dot(lhs, xt[rhs_rows, :])
            for i in range(4):
                put(pl.ds(start_row(zz, i // 2, i % 2, r0), n), res[i * n : (i + 1) * n], part == 0)
            return 0

        lax.fori_loop(0, 4, body, 0)

    def chunk_y(part):
        first = part < 2
        _, r0, n, _ = W_PIECES[1]
        yy = lax.rem(y + shift("y", part), 4)
        hi, lo = yy // 2, yy % 2
        rhs = jnp.concatenate(
            [xt[pl.ds(pl.multiple_of(xx * 768 + hi * 384, 384), 384), :] for xx in range(4)], axis=0
        )

        def body(zp, _):
            lhs = jnp.concatenate(
                [
                    jnp.concatenate([wbuf[xx, zp * 2 + zz, yy, cc, r0 : r0 + n, :] for xx in range(4)], axis=1)
                    for zz in range(2)
                    for cc in range(2)
                ],
                axis=0,
            )
            res = dot(lhs, rhs)
            for i in range(4):
                put(pl.ds(start_row(zp * 2 + i // 2, lo, i % 2, r0), n), res[i * n : (i + 1) * n], first)
            return 0

        lax.fori_loop(0, 2, body, 0)

    def chunk_z(part):
        _, r0, n, _ = W_PIECES[2]
        zz = lax.rem(z + shift("z", part), 4)
        lhs = jnp.concatenate(
            [
                jnp.concatenate(
                    [wbuf[xx, zz, yh * 2 + l, cc, r0 : r0 + n, :] for xx in range(4) for yh in range(2)], axis=1
                )
                for l in range(2)
                for cc in range(2)
            ],
            axis=0,
        )
        res = dot(lhs, xt[...])
        for i in range(4):
            put(pl.ds(start_row(zz, i // 2, i % 2, r0), n), res[i * n : (i + 1) * n], True)

    def chunk(part):
        chunk_x(part)
        chunk_y(part)
        chunk_z(part)

    each(ws, "crossed", 0)
    chunk(0)
    each(ws, "crossed", 1)
    chunk(1)
    each(ws, "third_far", 0)
    each(ws, "across", 3, 0)
    each(ws, "crossed", 2)
    chunk(2)
    for group in (1, 2, 3):
        each(ws, "third_far", group)
        each(ws, "across", 3, group)
    for group in range(4):
        each(ws, "crossed", 3, group)
    chunk(3)
    loads[7].wait()
    loads[8].wait()

    def unit(rows, gain):
        wide = acc[rows, :].astype(BF).astype(F32)
        scale = lax.rsqrt(jnp.sum(wide * wide, axis=0, keepdims=True) * (1.0 / 128) + 1e-06)
        return (wide * scale * gain).astype(BF)

    def column(gain):
        return jnp.concatenate([jnp.broadcast_to(gain[...], (128, 128)).T] * 3, axis=1)

    qcol, kcol = column(qg), column(kg)
    ii = lax.broadcasted_iota(jnp.int32, (128, 128), 0)
    jj = lax.broadcasted_iota(jnp.int32, (128, 128), 1)
    same = (ii >> 4) == (jj >> 4)

    def temporal(h, _):
        rows = pl.multiple_of(h * 128, 128)
        q = unit(pl.ds(rows, 128), qcol)
        k = unit(pl.ds(1536 + rows, 128), kcol)
        v = acc[pl.ds(3072 + rows, 128), :].astype(BF)
        for g in range(3):
            cols = slice(g * 128, (g + 1) * 128)
            s = dot(k[:, cols].T, q[:, cols]) * (128**-0.5)
            s = jnp.where(same, s, -1e30)
            e = jnp.exp(s - jnp.max(s, axis=0, keepdims=True))
            p = (e / jnp.sum(e, axis=0, keepdims=True)).astype(BF)
            ot[pl.ds(rows, 128), cols] = dot(v[:, cols], p).astype(BF)
        return 0

    lax.fori_loop(0, 12, temporal, 0)

    for copy in pending:
        copy.wait_send()

    def sent(i, _):
        t = lax.rem(chip + 1 + i, 8)
        rows = pl.ds(pl.multiple_of(t * 48, 16), 48)
        remote(mix.at[rows, :], moved.at[seq], a2a_s.at[i], a2a_r.at[i], other_chip(t)).wait_send()
        return 0

    lax.fori_loop(0, 7, sent, 0)

    def sent_near(i, _):
        to_near_rows(i).wait_send()
        return 0

    lax.fori_loop(0, 8, sent_near, 0)


def untangle(ot, out):
    a = lax.broadcasted_iota(jnp.int32, (128, 384), 0) + pl.program_id(0) * 128
    b = lax.broadcasted_iota(jnp.int32, (128, 384), 1)
    back = (a == (b & 15) * 24 + (b >> 4)).astype(F32).astype(BF)
    out[...] = lax.dot_general(back, ot[...], (((1,), (1,)), ((), ())), preferred_element_type=F32).astype(BF)


def local(
    tokens, spatial_query, spatial_key, spatial_value, out_weight, qkv_weight, modulation, query_gain, key_gain
):
    hbm = pl.BlockSpec(memory_space=pl.ANY)
    dma = pltpu.SemaphoreType.DMA
    turned = pl.pallas_call(
        kernel,
        out_shape=jax.ShapeDtypeStruct((1536, 384), BF),
        in_specs=[hbm] * 9,
        out_specs=pl.BlockSpec(memory_space=pltpu.VMEM),
        scratch_shapes=[
            pltpu.VMEM((192, 192), BF),
            pltpu.VMEM((72, 128), F32),
            pltpu.VMEM((8, 3072), F32),
            pltpu.VMEM((1, 128), F32),
            pltpu.VMEM((1, 128), F32),
            pltpu.VMEM((4, 4, 4, 2, 288, 384), BF),
            pltpu.VMEM((4, 4, 4, 2, 96, 384), BF),
            pltpu.VMEM((4608, 384), F32),
            pltpu.VMEM((384, 3072), BF),
            pltpu.VMEM((384, 1536), BF),
            pltpu.VMEM((384, 1536), BF),
            pltpu.VMEM((384, 1536), BF),
            pltpu.VMEM((384, 3072), BF),
            pltpu.VMEM((16, 48, 3072), BF),
            pltpu.VMEM((3072, 384), BF),
            pltpu.VMEM((96, 192), BF),
            dma((9,)),
            dma((6, 25)),
            dma((6, 25)),
            dma((6, 7)),
            dma((6, 7)),
            dma,
            dma,
            dma((7,)),
            dma((7,)),
            dma((8,)),
            dma((8,)),
        ],
        compiler_params=pltpu.CompilerParams(
            collective_id=0, has_side_effects=True, vmem_limit_bytes=62 * 2**20
        ),
        name="video_block",
    )(
        spatial_query.reshape(384, 1536),
        spatial_key.reshape(384, 1536),
        spatial_value.reshape(384, 1536),
        tokens.reshape(384, 3072),
        out_weight,
        qkv_weight.T,
        modulation.reshape(72, 128),
        query_gain.reshape(1, 128),
        key_gain.reshape(1, 128),
    )
    out = pl.pallas_call(
        untangle,
        out_shape=jax.ShapeDtypeStruct((384, 1536), BF),
        grid=(3,),
        in_specs=[pl.BlockSpec(memory_space=pltpu.VMEM)],
        out_specs=pl.BlockSpec((128, 1536), lambda i: (i, 0)),
        name="frame_major",
    )(turned)
    return out.reshape(1, 16, 24, 1536)


def solution(mesh):
    placed = (
        P("dp", "seq", None, None),
        P("dp", "seq", None, None),
        P("dp", "seq", None, None),
        P("dp", "seq", None, None),
        P("dp", "seq"),
        P("dp", "seq"),
        P("dp", None, None),
        P(),
        P(),
    )
    return jax.shard_map(
        local, mesh=mesh, in_specs=placed, out_specs=P("dp", None, "seq", None), check_vma=False
    )
```

time: 164 us -> 138 us (0.84); the launches traced: 164 us -> 136 us
  Pallas kernels: 157 us -> 136 us
  local copies, waits for them, and re-layouts: 6.52 us -> 0 us
    pallas_call x1 -> x2, Pallas kernels: 157 us -> 136 us  [the longest x1 133 us: local(): pl.pallas_call(kernel, out_shape=jax.ShapeDtypeStruct((1536, 384), BF), i...]
    unnamed x2 -> x0, local copies, waits for them, and re-layouts: 3.76 us -> none
    reshape x2 -> x0, local copies, waits for them, and re-layouts: 2.77 us -> none  [the longest x1 1.39 us: local(): query_gain.reshape(128, 1)]
where the time goes in v2:
time: 138 us; the launch traced here: 136 us
  Pallas kernels  136 us (99%)
    pallas_call x1, Pallas kernels, local(): pl.pallas_call(kernel, out_shape=jax.ShapeDtypeStruct((1536, 384), BF), i...  133 us
    pallas_call x1, Pallas kernels, local(): pl.pallas_call(untangle, out_shape=jax.ShapeDtypeStruct((384, 1536), BF),...  3.79 us

profile of v2, /device:TPU:1, one launch (start us, length us, event | category | flops | bytes accessed | tf_op | source)
XLA Modules:
  0.0 136.3 jit_solution(17729462116300096872)
XLA Ops:
  0.0 132.5 %video_block.1.ot = bf16[1536,384]{1,0:T(8,128)(2,1)} custom-call(bf16[384,1536]{1,0:T(8,128)(2,1)} %bitcast.10, bf16[384,1536]{1,0:T(8,128)(2,1)} %bitcast.11, bf16[384,1536]{1,0:T(8,128)(2,1)} %bitcast.12, bf16[384,3072]{1,0:T(8,128)(2,1)} %bitcast.9, bf16[192,192]{1,0:T(8,128)(2,1)} %ow_hbm.1, bf16[288,384]{1,0:T(8,128)(2,1)} %bitcast.13, ...), custom_call_target="tpu_custom_call" | custom-call | tf_op jit(solution)/shard_map/video_block/pallas_call | solution.py:495
  132.5 3.8 %frame_major.1 = bf16[384,1536]{1,0:T(8,128)(2,1)} custom-call(bf16[1536,384]{1,0:T(8,128)(2,1)} %video_block.1.ot), custom_call_target="tpu_custom_call" | custom-call | tf_op jit(solution)/shard_map/frame_major/pallas_call | solution.py:544

commit v3 on v2

--- a/solution.py
+++ b/solution.py
@@ -124,10 +124,9 @@
             for part in (1, 2, 3):
                 self.wait(self.slot(0, part), part - 1)
 
-        def second(self):
+        def second(self, k):
             axis = self.order[1]
-            for k in range(2):
-                for way in range(2):
+            for way in range(2):
                     self.send(self.slot(1, 0, "AB"[(way + k) % 2]), 3 + way * 3 + k, to(axis, way))
 
         def second_on(self):
@@ -220,38 +219,37 @@
 
     heads(0, 2)
     each(os, "first_done")
-    each(os, "second")
+    each(os, "second", 0)
+    each(os, "second", 1)
     each(os, "third", 0)
     each(ws, "first_done")
-    each(ws, "second")
     heads(2, 2)
     each(os, "second_on")
-    heads(4, 2)
+    heads(4, 3)
     each(os, "second_sides")
     each(os, "third", 1)
     each(os, "third", 2)
-    each(ws, "second_on")
-    heads(6, 2)
+    heads(7, 2)
     each(os, "second_far")
     each(os, "third", 3)
     each(os, "across", 0)
+    each(ws, "second", 0)
+    each(ws, "second", 1)
+    heads(9, 3)
+    each(os, "third_on", 0)
     each(ws, "third", 0)
-    heads(8, 2)
-    each(os, "third_on", 0)
-    heads(10, 2)
     each(os, "third_on", 1)
     each(os, "third_on", 2)
-    each(ws, "second_sides")
-    each(ws, "second_far")
     each(os, "third_on", 3)
-    for group in (1, 2, 3):
-        each(ws, "third", group)
     each(os, "across", 1)
     each(os, "across", 2)
+    each(ws, "second_on")
     for group in range(4):
         each(os, "third_far", group)
         each(os, "across", 3, group)
-    each(ws, "across", 0)
+    each(ws, "second_sides")
+    each(ws, "third", 1)
+    each(ws, "third", 2)
     for part in range(3):
         each(os, "crossed", part)
     for group in range(4):
@@ -274,70 +272,81 @@
         )
         cols = pl.ds(pl.multiple_of(zz * 768, 768), 768)
         proj = dot(qs[...], rhs)
-        mix[:, cols] = (tok[:, cols].astype(F32) + mod[0:1, cols] * proj).astype(BF)
+        mix[zz] = (tok[:, cols].astype(F32) + mod[0:1, cols] * proj).astype(BF)
         return 0
 
     lax.fori_loop(0, 4, project, 0)
+    each(ws, "second_far")
+    each(ws, "third", 3)
+    each(ws, "across", 0)
     each(ws, "third_on", 0)
 
     def normed(t):
         rows = pl.ds(pl.multiple_of(t * 48, 16), 48)
-        wide = mix[rows, :].astype(F32)
+        wide = jnp.concatenate([mix[i, rows, :] for i in range(4)], axis=1).astype(F32)
         mean = jnp.mean(wide, axis=1, keepdims=True)
         dev = wide - mean
         var = jnp.mean(dev * dev, axis=1, keepdims=True)
         return rows, (dev * lax.rsqrt(var + 1e-06) * (1.0 + mod[2:3, :]) + mod[1:2, :]).astype(BF)
 
-    def norm_and_send(i, _):
+    def norm(i, _):
+        rows, value = normed(i)
+        for block in range(4):
+            mix[block, rows, :] = value[:, block * 768 : (block + 1) * 768]
+        return 0
+
+    lax.fori_loop(0, 8, norm, 0)
+
+    def features(block):
+        return lax.rem(x + shift("x", block), 4)
+
+    def leave(block, i):
         t = lax.rem(chip + 1 + i, 8)
-        rows, value = normed(t)
-        mix[rows, :] = value
-        remote(mix.at[rows, :], moved.at[seq], a2a_s.at[i], a2a_r.at[i], other_chip(t)).start()
-        return 0
-
-    lax.fori_loop(0, 7, norm_and_send, 0)
-    each(ws, "third_on", 1)
-    each(ws, "third_on", 2)
-    moved[seq] = normed(chip)[1]
-
-    def to_near_rows(i):
+        rows = pl.ds(pl.multiple_of(t * 48, 16), 48)
+        src, dst = mix.at[features(block), rows, :], moved.at[features(block), seq]
+        return remote(src, dst, a2a_s.at[block, i], a2a_r.at[block, i], other_chip(t))
+
+    def over(block, i, core):
         t = lax.rem(chip + 7 - i, 8)
-        ref = moved.at[t * 2 + c, pl.ds(pl.multiple_of(16 * (1 - c), 16), 32), :]
-        return remote(ref, ref, fwd_s.at[i], fwd_r.at[i], near)
-
-    to_near_rows(7).start()
-    each(ws, "third_on", 3)
-    each(ws, "across", 1)
-    each(ws, "across", 2)
-
-    def pass_on(i, _):
-        t = lax.rem(chip + 7 - i, 8)
-        ref = moved.at[t * 2 + c]
-        remote(ref, ref, a2a_s.at[i], a2a_r.at[i], near).wait_recv()
-        to_near_rows(i).start()
-        return 0
-
-    lax.fori_loop(0, 7, pass_on, 0)
-
-    def arrive(i, _):
-        t = lax.rem(chip + 7 - i, 8)
-        ref = moved.at[t * 2 + 1 - c, pl.ds(pl.multiple_of(16 * c, 16), 32), :]
-        remote(ref, ref, fwd_s.at[i], fwd_r.at[i], near).wait_recv()
-        return 0
-
-    lax.fori_loop(0, 8, arrive, 0)
+        rows = pl.ds(pl.multiple_of(16 * (1 - core), 16), 32)
+        ref = moved.at[features(block), t * 2 + core, rows, :]
+        return remote(ref, ref, fwd_s.at[block, i], fwd_r.at[block, i], near)
+
+    def times(count, body):
+        def run(i, _):
+            body(i)
+            return 0
+
+        lax.fori_loop(0, count, run, 0)
+
+    for block in range(4):
+        times(7, lambda i: leave(block, i).start())
+    for block in range(4):
+        moved[block, seq] = mix[block, pl.ds(pl.multiple_of(chip * 48, 16), 48), :]
+    for block in range(4):
+        over(block, 7, c).start()
 
     m = lax.broadcasted_iota(jnp.int32, (384, 512), 0)
     r = lax.broadcasted_iota(jnp.int32, (384, 512), 1)
     pick = (r == (m & 15) * 32 + (m >> 4) + 8 * c).astype(F32).astype(BF)
 
-    def turn(i, _):
-        cols = pl.ds(pl.multiple_of(i * 384, 384), 384)
-        rows = moved[:, pl.ds(pl.multiple_of(16 * c, 16), 32), cols].reshape(512, 384)
-        xt[cols, :] = dot(pick, rows).astype(BF).T
-        return 0
-
-    lax.fori_loop(0, 8, turn, 0)
+    def gather_block(block):
+        def one(i):
+            t = lax.rem(chip + 7 - i, 8)
+            ref = moved.at[features(block), t * 2 + c]
+            remote(ref, ref, a2a_s.at[block, i], a2a_r.at[block, i], near).wait_recv()
+            over(block, i, c).start()
+
+        times(7, one)
+        times(8, lambda i: over(block, i, 1 - c).wait_recv())
+
+        def turn(i):
+            inner = pl.ds(pl.multiple_of(i * 384, 384), 384)
+            rows = moved[features(block), :, pl.ds(pl.multiple_of(16 * c, 16), 32), inner].reshape(512, 384)
+            at = pl.ds(pl.multiple_of(features(block) * 768 + i * 384, 384), 384)
+            xt[at, :] = dot(pick, rows).astype(BF).T
+
+        times(2, turn)
 
     def put(rows, value, first):
         if first:
@@ -348,7 +357,7 @@
     def start_row(zz, l, cc, r0):
         return pl.multiple_of(zz * 1152 + l * 576 + cc * 288 + r0, 16)
 
-    def chunk_x(part):
+    def chunk_x(part, group=None):
         _, r0, n, _ = W_PIECES[0]
         xx = lax.rem(x + shift("x", part), 4)
         rhs_rows = pl.ds(pl.multiple_of(xx * 768, 768), 768)
@@ -367,7 +376,10 @@
                 put(pl.ds(start_row(zz, i // 2, i % 2, r0), n), res[i * n : (i + 1) * n], part == 0)
             return 0
 
-        lax.fori_loop(0, 4, body, 0)
+        if group is None:
+            lax.fori_loop(0, 4, body, 0)
+        else:
+            body(lax.rem(z + shift("z", group), 4), 0)
 
     def chunk_y(part):
         first = part < 2
@@ -411,25 +423,44 @@
         for i in range(4):
             put(pl.ds(start_row(zz, i // 2, i % 2, r0), n), res[i * n : (i + 1) * n], True)
 
-    def chunk(part):
-        chunk_x(part)
-        chunk_y(part)
-        chunk_z(part)
-
+    each(ws, "third_on", 1)
+    each(ws, "third_on", 2)
+    gather_block(0)
     each(ws, "crossed", 0)
-    chunk(0)
+    chunk_x(0)
+    each(ws, "third_on", 3)
+    each(ws, "across", 1)
+    each(ws, "across", 2)
+    gather_block(1)
     each(ws, "crossed", 1)
-    chunk(1)
+    chunk_x(1)
+    gather_block(2)
+    each(ws, "crossed", 2)
+    chunk_x(2)
     each(ws, "third_far", 0)
     each(ws, "across", 3, 0)
-    each(ws, "crossed", 2)
-    chunk(2)
-    for group in (1, 2, 3):
-        each(ws, "third_far", group)
-        each(ws, "across", 3, group)
+    gather_block(3)
+    chunk_y(0)
+    chunk_z(0)
+    each(ws, "third_far", 1)
+    each(ws, "across", 3, 1)
+    chunk_y(1)
+    chunk_z(1)
+    each(ws, "third_far", 2)
+    each(ws, "across", 3, 2)
+    chunk_y(2)
+    chunk_z(2)
+    each(ws, "third_far", 3)
+    each(ws, "across", 3, 3)
+    for group in range(3):
+        each(ws[:1], "crossed", 3, group)
+        chunk_x(3, group)
     for group in range(4):
-        each(ws, "crossed", 3, group)
-    chunk(3)
+        each(ws[1:], "crossed", 3, group)
+    chunk_y(3)
+    chunk_z(3)
+    each(ws[:1], "crossed", 3, 3)
+    chunk_x(3, 3)
     loads[7].wait()
     loads[8].wait()
 
@@ -446,7 +477,7 @@
     jj = lax.broadcasted_iota(jnp.int32, (128, 128), 1)
     same = (ii >> 4) == (jj >> 4)
 
-    def temporal(h, _):
+    def temporal(h):
         rows = pl.multiple_of(h * 128, 128)
         q = unit(pl.ds(rows, 128), qcol)
         k = unit(pl.ds(1536 + rows, 128), kcol)
@@ -458,26 +489,20 @@
             e = jnp.exp(s - jnp.max(s, axis=0, keepdims=True))
             p = (e / jnp.sum(e, axis=0, keepdims=True)).astype(BF)
             ot[pl.ds(rows, 128), cols] = dot(v[:, cols], p).astype(BF)
+
+    def two_heads(i, _):
+        temporal(i * 2)
+        temporal(i * 2 + 1)
         return 0
 
-    lax.fori_loop(0, 12, temporal, 0)
+    lax.fori_loop(0, 6, two_heads, 0)
 
     for copy in pending:
         copy.wait_send()
 
-    def sent(i, _):
-        t = lax.rem(chip + 1 + i, 8)
-        rows = pl.ds(pl.multiple_of(t * 48, 16), 48)
-        remote(mix.at[rows, :], moved.at[seq], a2a_s.at[i], a2a_r.at[i], other_chip(t)).wait_send()
-        return 0
-
-    lax.fori_loop(0, 7, sent, 0)
-
-    def sent_near(i, _):
-        to_near_rows(i).wait_send()
-        return 0
-
-    lax.fori_loop(0, 8, sent_near, 0)
+    for block in range(4):
+        times(7, lambda i: leave(block, i).wait_send())
+        times(8, lambda i: over(block, i, c).wait_send())
 
 
 def untangle(ot, out):
@@ -510,8 +535,8 @@
             pltpu.VMEM((384, 1536), BF),
             pltpu.VMEM((384, 1536), BF),
             pltpu.VMEM((384, 1536), BF),
-            pltpu.VMEM((384, 3072), BF),
-            pltpu.VMEM((16, 48, 3072), BF),
+            pltpu.VMEM((4, 384, 768), BF),
+            pltpu.VMEM((4, 16, 48, 768), BF),
             pltpu.VMEM((3072, 384), BF),
             pltpu.VMEM((96, 192), BF),
             dma((9,)),
@@ -521,10 +546,10 @@
             dma((6, 7)),
             dma,
             dma,
-            dma((7,)),
-            dma((7,)),
-            dma((8,)),
-            dma((8,)),
+            dma((4, 7)),
+            dma((4, 7)),
+            dma((4, 8)),
+            dma((4, 8)),
         ],
         compiler_params=pltpu.CompilerParams(
             collective_id=0, has_side_effects=True, vmem_limit_bytes=62 * 2**20

time: 138 us -> 132 us (0.957); the launches traced: 136 us -> 132 us
  Pallas kernels: 136 us -> 132 us
    pallas_call x1, Pallas kernels: 133 us -> 128 us  [local(): pl.pallas_call(kernel, out_shape=jax.ShapeDtypeStruct((1536, 384), BF), i...]
where the time goes in v3:
time: 132 us
  Pallas kernels  132 us (100%)
    pallas_call x1, Pallas kernels, local(): pl.pallas_call(kernel, out_shape=jax.ShapeDtypeStruct((1536, 384), BF), i...  128 us
    pallas_call x1, Pallas kernels, local(): pl.pallas_call(untangle, out_shape=jax.ShapeDtypeStruct((384, 1536), BF),...  3.79 us

profile of v3, /device:TPU:1, one launch (start us, length us, event | category | flops | bytes accessed | tf_op | source)
XLA Modules:
  0.0 131.9 jit_solution(18424417983929085115)
XLA Ops:
  0.0 128.1 %video_block.1.ot = bf16[1536,384]{1,0:T(8,128)(2,1)} custom-call(bf16[384,1536]{1,0:T(8,128)(2,1)} %bitcast.10, bf16[384,1536]{1,0:T(8,128)(2,1)} %bitcast.11, bf16[384,1536]{1,0:T(8,128)(2,1)} %bitcast.12, bf16[384,3072]{1,0:T(8,128)(2,1)} %bitcast.9, bf16[192,192]{1,0:T(8,128)(2,1)} %ow_hbm.1, bf16[288,384]{1,0:T(8,128)(2,1)} %bitcast.13, ...), custom_call_target="tpu_custom_call" | custom-call | tf_op jit(solution)/shard_map/video_block/pallas_call | solution.py:520
  128.1 3.8 %frame_major.1 = bf16[384,1536]{1,0:T(8,128)(2,1)} custom-call(bf16[1536,384]{1,0:T(8,128)(2,1)} %video_block.1.ot), custom_call_target="tpu_custom_call" | custom-call | tf_op jit(solution)/shard_map/frame_major/pallas_call | solution.py:569

commit v4 on v2

--- a/solution.py
+++ b/solution.py
@@ -124,10 +124,9 @@
             for part in (1, 2, 3):
                 self.wait(self.slot(0, part), part - 1)
 
-        def second(self):
+        def second(self, k):
             axis = self.order[1]
-            for k in range(2):
-                for way in range(2):
+            for way in range(2):
                     self.send(self.slot(1, 0, "AB"[(way + k) % 2]), 3 + way * 3 + k, to(axis, way))
 
         def second_on(self):
@@ -220,38 +219,37 @@
 
     heads(0, 2)
     each(os, "first_done")
-    each(os, "second")
+    each(os, "second", 0)
+    each(os, "second", 1)
     each(os, "third", 0)
     each(ws, "first_done")
-    each(ws, "second")
     heads(2, 2)
     each(os, "second_on")
-    heads(4, 2)
+    heads(4, 3)
     each(os, "second_sides")
     each(os, "third", 1)
     each(os, "third", 2)
-    each(ws, "second_on")
-    heads(6, 2)
+    heads(7, 2)
     each(os, "second_far")
     each(os, "third", 3)
     each(os, "across", 0)
+    each(ws, "second", 0)
+    each(ws, "second", 1)
+    heads(9, 3)
+    each(os, "third_on", 0)
     each(ws, "third", 0)
-    heads(8, 2)
-    each(os, "third_on", 0)
-    heads(10, 2)
     each(os, "third_on", 1)
     each(os, "third_on", 2)
-    each(ws, "second_sides")
-    each(ws, "second_far")
     each(os, "third_on", 3)
-    for group in (1, 2, 3):
-        each(ws, "third", group)
     each(os, "across", 1)
     each(os, "across", 2)
+    each(ws, "second_on")
     for group in range(4):
         each(os, "third_far", group)
         each(os, "across", 3, group)
-    each(ws, "across", 0)
+    each(ws, "second_sides")
+    each(ws, "third", 1)
+    each(ws, "third", 2)
     for part in range(3):
         each(os, "crossed", part)
     for group in range(4):
@@ -278,6 +276,9 @@
         return 0
 
     lax.fori_loop(0, 4, project, 0)
+    each(ws, "second_far")
+    each(ws, "third", 3)
+    each(ws, "across", 0)
     each(ws, "third_on", 0)
 
     def normed(t):
@@ -348,7 +349,7 @@
     def start_row(zz, l, cc, r0):
         return pl.multiple_of(zz * 1152 + l * 576 + cc * 288 + r0, 16)
 
-    def chunk_x(part):
+    def chunk_x(part, group=None):
         _, r0, n, _ = W_PIECES[0]
         xx = lax.rem(x + shift("x", part), 4)
         rhs_rows = pl.ds(pl.multiple_of(xx * 768, 768), 768)
@@ -367,7 +368,10 @@
                 put(pl.ds(start_row(zz, i // 2, i % 2, r0), n), res[i * n : (i + 1) * n], part == 0)
             return 0
 
-        lax.fori_loop(0, 4, body, 0)
+        if group is None:
+            lax.fori_loop(0, 4, body, 0)
+        else:
+            body(lax.rem(z + shift("z", group), 4), 0)
 
     def chunk_y(part):
         first = part < 2
@@ -393,6 +397,58 @@
             return 0
 
         lax.fori_loop(0, 2, body, 0)
+
+    def near_x():
+        _, r0, n, _ = W_PIECES[0]
+        places = [lax.rem(x + shift("x", part), 4) for part in range(3)]
+        rhs = jnp.concatenate([xt[pl.ds(pl.multiple_of(xx * 768, 768), 768), :] for xx in places], axis=0)
+
+        def body(i, _):
+            zz, l = i // 2, i % 2
+            lhs = jnp.concatenate(
+                [
+                    jnp.concatenate(
+                        [wbuf[xx, zz, yh * 2 + l, cc, r0 : r0 + n, :] for xx in places for yh in range(2)], axis=1
+                    )
+                    for cc in range(2)
+                ],
+                axis=0,
+            )
+            res = dot(lhs, rhs)
+            for cc in range(2):
+                put(pl.ds(start_row(zz, l, cc, r0), n), res[cc * n : (cc + 1) * n], True)
+            return 0
+
+        lax.fori_loop(0, 8, body, 0)
+
+    def sides_y():
+        _, r0, n, _ = W_PIECES[1]
+        places = [lax.rem(y + shift("y", part), 4) for part in (1, 2)]
+        rhs = jnp.concatenate(
+            [
+                xt[pl.ds(pl.multiple_of(xx * 768 + yy // 2 * 384, 384), 384), :]
+                for yy in places
+                for xx in range(4)
+            ],
+            axis=0,
+        )
+
+        def body(zz, _):
+            lhs = jnp.concatenate(
+                [
+                    jnp.concatenate(
+                        [wbuf[xx, zz, yy, cc, r0 : r0 + n, :] for yy in places for xx in range(4)], axis=1
+                    )
+                    for cc in range(2)
+                ],
+                axis=0,
+            )
+            res = dot(lhs, rhs)
+            for cc in range(2):
+                put(pl.ds(start_row(zz, 1 - yl, cc, r0), n), res[cc * n : (cc + 1) * n], True)
+            return 0
+
+        lax.fori_loop(0, 4, body, 0)
 
     def chunk_z(part):
         _, r0, n, _ = W_PIECES[2]
@@ -411,25 +467,30 @@
         for i in range(4):
             put(pl.ds(start_row(zz, i // 2, i % 2, r0), n), res[i * n : (i + 1) * n], True)
 
-    def chunk(part):
-        chunk_x(part)
-        chunk_y(part)
-        chunk_z(part)
-
-    each(ws, "crossed", 0)
-    chunk(0)
-    each(ws, "crossed", 1)
-    chunk(1)
+    for part in range(3):
+        each(ws, "crossed", part)
     each(ws, "third_far", 0)
     each(ws, "across", 3, 0)
-    each(ws, "crossed", 2)
-    chunk(2)
-    for group in (1, 2, 3):
-        each(ws, "third_far", group)
-        each(ws, "across", 3, group)
+    near_x()
+    each(ws, "third_far", 1)
+    each(ws, "across", 3, 1)
+    chunk_y(0)
+    sides_y()
+    each(ws, "third_far", 2)
+    each(ws, "across", 3, 2)
+    for part in range(3):
+        chunk_z(part)
+    each(ws, "third_far", 3)
+    each(ws, "across", 3, 3)
+    for group in range(3):
+        each(ws[:1], "crossed", 3, group)
+        chunk_x(3, group)
     for group in range(4):
-        each(ws, "crossed", 3, group)
-    chunk(3)
+        each(ws[1:], "crossed", 3, group)
+    chunk_y(3)
+    chunk_z(3)
+    each(ws[:1], "crossed", 3, 3)
+    chunk_x(3, 3)
     loads[7].wait()
     loads[8].wait()
 
@@ -446,7 +507,7 @@
     jj = lax.broadcasted_iota(jnp.int32, (128, 128), 1)
     same = (ii >> 4) == (jj >> 4)
 
-    def temporal(h, _):
+    def temporal(h):
         rows = pl.multiple_of(h * 128, 128)
         q = unit(pl.ds(rows, 128), qcol)
         k = unit(pl.ds(1536 + rows, 128), kcol)
@@ -458,9 +519,13 @@
             e = jnp.exp(s - jnp.max(s, axis=0, keepdims=True))
             p = (e / jnp.sum(e, axis=0, keepdims=True)).astype(BF)
             ot[pl.ds(rows, 128), cols] = dot(v[:, cols], p).astype(BF)
-        return 0
-
-    lax.fori_loop(0, 12, temporal, 0)
+
+    def two_heads(i, _):
+        temporal(i * 2)
+        temporal(i * 2 + 1)
+        return 0
+
+    lax.fori_loop(0, 6, two_heads, 0)
 
     for copy in pending:
         copy.wait_send()

time: 138 us -> 131 us (0.949)
  Pallas kernels: 136 us -> 130 us
    pallas_call x1, Pallas kernels: 133 us -> 127 us  [local(): pl.pallas_call(kernel, out_shape=jax.ShapeDtypeStruct((1536, 384), BF), i...]
where the time goes in v4:
time: 131 us; the launch traced here: 130 us
  Pallas kernels  130 us (99%)
    pallas_call x1, Pallas kernels, local(): pl.pallas_call(kernel, out_shape=jax.ShapeDtypeStruct((1536, 384), BF), i...  127 us
    pallas_call x1, Pallas kernels, local(): pl.pallas_call(untangle, out_shape=jax.ShapeDtypeStruct((384, 1536), BF),...  3.79 us

profile of v4, /device:TPU:1, one launch (start us, length us, event | category | flops | bytes accessed | tf_op | source)
XLA Modules:
  0.0 130.4 jit_solution(4244567549606779665)
XLA Ops:
  0.0 126.6 %video_block.1.ot = bf16[1536,384]{1,0:T(8,128)(2,1)} custom-call(bf16[384,1536]{1,0:T(8,128)(2,1)} %bitcast.10, bf16[384,1536]{1,0:T(8,128)(2,1)} %bitcast.11, bf16[384,1536]{1,0:T(8,128)(2,1)} %bitcast.12, bf16[384,3072]{1,0:T(8,128)(2,1)} %bitcast.9, bf16[192,192]{1,0:T(8,128)(2,1)} %ow_hbm.1, bf16[288,384]{1,0:T(8,128)(2,1)} %bitcast.13, ...), custom_call_target="tpu_custom_call" | custom-call | tf_op jit(solution)/shard_map/video_block/pallas_call | solution.py:560
  126.6 3.8 %frame_major.1 = bf16[384,1536]{1,0:T(8,128)(2,1)} custom-call(bf16[1536,384]{1,0:T(8,128)(2,1)} %video_block.1.ot), custom_call_target="tpu_custom_call" | custom-call | tf_op jit(solution)/shard_map/frame_major/pallas_call | solution.py:609
